TPU v7x, 512 devices: a whole 4x8x8 slice. The times are simulated.
512 devices in a mesh: ctx: 16 (over x, z_hi), dp: 8 (over y), tp: 4 (over z_lo, core).
Axes of the slice: x: 4, y: 8, z: 8 (z_hi: 4, z_lo: 2; z = z_hi * 2 + z_lo), core: 2. Of those that a mesh axis runs over, the one named last changes fastest.
Arguments:
- token_ids: int32 [4, 16], replicated, may hold values from 0 to 50279
- decode_prompt: int32 [16], replicated, may hold values from 0 to 15, as said below
- embedding: bfloat16 [50280, 4096], P('dp', ('ctx', 'tp')), may hold values from -6 to 6
- norm_gain: float32 [4096], replicated, may hold values from 0.1 to 1.9
- w_zx: bfloat16 [2, 128, 64, 4096], P(None, ('tp', 'ctx')), may hold values from -0.09375 to 0.09375
- w_bcdt: bfloat16 [4096, 384], P(None, ('ctx', 'tp')), may hold values from -0.09375 to 0.09375
- conv_x_weight: float32 [4, 128, 64], P(None, ('tp', 'ctx')), may hold values from -3 to 3
- conv_x_bias: float32 [128, 64], P(('tp', 'ctx')), may hold values from -3 to 3
- conv_bc_weight: float32 [4, 256], replicated, may hold values from -3 to 3
- conv_bc_bias: float32 [256], replicated, may hold values from -3 to 3
- dt_bias: float32 [128], P(('tp', 'ctx')), may hold values from -4 to -1
- a_log: float32 [128], P(('tp', 'ctx')), may hold values from 0 to 2.7
- d_skip: float32 [128], P(('tp', 'ctx')), may hold values from 0.5 to 1.5
- gate_norm_gain: float32 [128, 64], P(('tp', 'ctx')), may hold values from 0.1 to 1.9
- w_out: bfloat16 [128, 64, 4096], P(('tp', 'ctx')), may hold values from -0.0625 to 0.0625
- state_parts: bfloat16 [16, 16, 128, 64, 128], P('ctx', 'dp', 'tp'), may hold values from -6 to 6
- seg_rate: float32 [16, 16, 128], P('ctx', 'dp', 'tp'), may hold values from 0 to 2
- x_tail: bfloat16 [16, 3, 128, 64], P('dp', None, ('tp', 'ctx')), may hold values from -6 to 6
- bc_tail: bfloat16 [16, 3, 256], P('dp'), may hold values from -6 to 6
Outputs:
- mixer_out: bfloat16 [4, 16, 4096], P(None, 'dp', ('ctx', 'tp'))
- final_state: float32 [16, 128, 64, 128], P('dp', ('tp', 'ctx'))
Inputs may be any that keep to these rules, and one draw needn't show every extreme that they name: decode_prompt is a permutation of the prompts; slot s is decoded by dp group s // 2, and prompt q is held by dp group q // 2; the 2 prompts held by one dp group are decoded by 2 different dp groups.
All inputs are finite; a program needn't handle non-finite values.
Results may differ from a plain program's by a relative error of at most 0.02.
Values may be sent and summed in bfloat16 or wider, within the bound.
No kernel may reach another device: no remote copies, remote signals or barrier semaphores. Data moves between devices by JAX's collectives and lax.ppermute only.
A program may use at most 64 MiB of HBM per device.

v0:
```python
import jax
import jax.numpy as jnp
from jax import lax
from jax.sharding import PartitionSpec as P

HEADS = 128
HEAD_DIM = 64
EPS = 1e-05
BOTH = ("ctx", "tp")
BF = jnp.bfloat16
F32 = jnp.float32


def exchange(pieces, axis):
    return lax.all_to_all(pieces, axis, 0, 0, tiled=True)


def in_three(values):
    first = values.astype(BF)
    rest = values - first.astype(F32)
    second = rest.astype(BF)
    third = (rest - second.astype(F32)).astype(BF)
    return (first, second, third)


def per_device(
    token_ids,
    decode_prompt,
    embedding,
    norm_gain,
    w_zx,
    w_bcdt,
    conv_x_weight,
    conv_x_bias,
    conv_bc_weight,
    conv_bc_bias,
    dt_bias,
    a_log,
    d_skip,
    gate_norm_gain,
    w_out,
    state_parts,
    seg_rate,
    x_tail,
    bc_tail,
):
    ctx, group, tp = (lax.axis_index(a) for a in ("ctx", "dp", "tp"))
    n_ctx, n_dp, n_tp = (lax.axis_size(a) for a in ("ctx", "dp", "tp"))
    slots = state_parts.shape[1]
    heads = w_zx.shape[1]
    state_width = state_parts.shape[-1]
    steps = token_ids.shape[0]
    vocab_rows, features = embedding.shape
    model = norm_gain.shape[0]
    rows = steps * slots
    channels = heads * HEAD_DIM
    block = features * n_tp
    states = state_parts[0].reshape(slots, n_ctx, heads, HEAD_DIM, state_width)
    states = jnp.swapaxes(states, 0, 1).reshape(n_ctx, -1, state_width)
    own_columns = w_bcdt.shape[1]
    w_pieces = w_bcdt.T.reshape(own_columns, n_ctx, block)
    w_pieces = jnp.swapaxes(w_pieces, 0, 1).reshape(n_ctx, -1, state_width)
    rates = jnp.swapaxes(seg_rate[0].reshape(slots, n_ctx, heads), 0, 1)
    rates = jnp.stack(in_three(rates), axis=1).reshape(n_ctx, -1, 1)
    rates = jnp.broadcast_to(rates, (*rates.shape[:2], state_width))
    state_rows, w_rows, rate_rows = (states.shape[1], w_pieces.shape[1], rates.shape[1])
    sent = jnp.concatenate([states, w_pieces, rates], axis=1)
    filler = -sent.shape[1] % 16
    sent = jnp.pad(sent, ((0, 0), (0, filler), (0, 0)))
    got = exchange(sent, "ctx")
    prompts = decode_prompt.shape[0]
    chosen = (decode_prompt[:, None] == jnp.arange(prompts)[None, :]).astype(jnp.int32)
    tokens = jnp.sum(token_ids[:, None, :] * chosen[None], axis=2)
    tokens = jnp.swapaxes(tokens.reshape(steps, n_dp, slots), 0, 1).reshape(-1)
    hot = (tokens[:, None] - group * vocab_rows == jnp.arange(vocab_rows)[None, :]).astype(BF)
    found = jnp.dot(hot, embedding, preferred_element_type=F32).astype(BF)
    found = lax.psum(found, "dp")
    own = lax.dynamic_slice_in_dim(found, group * rows, rows)
    beside = lax.all_gather(own, "tp")
    near = jnp.swapaxes(beside, 0, 1).reshape(rows, block).astype(F32)
    near_gain = lax.dynamic_slice_in_dim(norm_gain, ctx * block, block)
    w_block = got[:, state_rows : state_rows + w_rows].reshape(-1, block)
    partial = lax.dot_general(
        (near * near_gain).astype(BF), w_block, (((1,), (1,)), ((), ())), preferred_element_type=F32
    ).astype(BF)
    piece = jnp.concatenate([own.reshape(-1, 128), partial.reshape(-1, 128)], axis=0)
    own_rows = own.size // 128
    everyone = exchange(jnp.broadcast_to(piece[None], (n_ctx * n_tp, *piece.shape)), BOTH)
    parts = got[:, state_rows + w_rows : state_rows + w_rows + rate_rows, 0].astype(F32)
    parts = parts.reshape(n_ctx, 3, slots, heads)
    rate = parts[:, 0] + parts[:, 1] + parts[:, 2]
    later = jnp.cumsum(rate[::-1], axis=0)[::-1] - rate
    weight = jnp.exp(-later)[..., None, None]
    scaled = weight * got[:, :state_rows].reshape(
        n_ctx, slots, heads, HEAD_DIM, state_width
    ).astype(F32)
    combined = jnp.sum(scaled.astype(BF).astype(F32), axis=0).astype(BF)
    bundle = jnp.concatenate(
        [
            combined.reshape(slots, -1, 128),
            jnp.swapaxes(x_tail, 1, 1).reshape(slots, -1, 128),
            bc_tail.reshape(slots, -1, 128),
        ],
        axis=1,
    )
    bundle = jnp.pad(bundle, ((0, 0), (0, -bundle.shape[1] % 16), (0, 0)))
    wanted = decode_prompt.reshape(n_dp, slots) - group * slots
    second = jnp.any(wanted == 1, axis=1)
    routed = jnp.where(second[:, None, None], bundle[1][None], bundle[0][None])
    arrived = exchange(routed, "dp")
    taken = everyone[:, :own_rows].reshape(n_ctx * n_tp, rows, features)
    flat = jnp.swapaxes(taken, 0, 1).reshape(rows, model).astype(F32)
    inverse = lax.rsqrt(jnp.mean(flat * flat, axis=-1, keepdims=True) + EPS)
    normed = (flat * inverse * norm_gain).astype(BF)
    projected = jnp.einsum("rd,khed->krhe", normed, w_zx, preferred_element_type=F32)
    projected = projected.reshape(2, steps, slots, heads, HEAD_DIM)
    sums = everyone[:, own_rows:].reshape(n_ctx, n_tp, rows, n_ctx, own_columns).astype(F32)
    sums = jnp.sum(sums, axis=0).transpose(1, 2, 0, 3).reshape(rows, -1)
    columns = (sums * inverse).reshape(steps, slots, -1)
    own_slots = lax.dynamic_slice_in_dim(decode_prompt, group * slots, slots)
    taken = jnp.stack(
        [
            lax.dynamic_index_in_dim(arrived, own_slots[s] // slots, 0, keepdims=False)
            for s in range(slots)
        ]
    ).astype(F32)
    at = combined.size // slots // 128
    ssm_state = taken[:, :at].reshape(slots, heads, HEAD_DIM, state_width)
    tail_rows = x_tail.size // slots // 128
    x_window = taken[:, at : at + tail_rows].reshape(slots, 3, heads, HEAD_DIM)
    bc_rows = bc_tail.size // slots // 128
    bc_window = taken[:, at + tail_rows : at + tail_rows + bc_rows].reshape(slots, 3, -1)
    head_start = 2 * state_width + (tp * n_ctx + ctx) * heads
    dt_raw = lax.dynamic_slice_in_dim(columns, head_start, heads, 2)
    decay_rate = -jnp.exp(a_log)
    gated_steps = []
    for moment in range(steps):
        x_window = jnp.concatenate([x_window, projected[1, moment][:, None]], axis=1)
        bc_window = jnp.concatenate(
            [bc_window, columns[moment, :, None, : 2 * state_width]], axis=1
        )
        x_conv = jax.nn.silu(jnp.einsum("pkhe,khe->phe", x_window, conv_x_weight) + conv_x_bias)
        bc_conv = jax.nn.silu(jnp.einsum("pkn,kn->pn", bc_window, conv_bc_weight) + conv_bc_bias)
        step_size = jax.nn.softplus(dt_raw[moment] + dt_bias)
        retain = jnp.exp(step_size * decay_rate)
        ssm_state = (
            retain[:, :, None, None] * ssm_state
            + (step_size[:, :, None] * x_conv)[:, :, :, None] * bc_conv[:, None, None, :state_width]
        )
        output = (
            jnp.einsum("phen,pn->phe", ssm_state, bc_conv[:, state_width:])
            + d_skip[None, :, None] * x_conv
        )
        gated_steps.append(output * jax.nn.silu(projected[0, moment]))
        x_window = x_window[:, 1:]
        bc_window = bc_window[:, 1:]
    gated = jnp.stack(gated_steps).reshape(rows, channels)
    squares = jnp.sum(gated * gated, axis=1)
    weighted = (gated * gate_norm_gain.reshape(-1)).astype(BF)
    partial_out = jnp.dot(weighted, w_out.reshape(channels, model), preferred_element_type=F32)
    partial_out = jnp.swapaxes(partial_out.reshape(rows, n_ctx * n_tp, -1), 0, 1)
    partial_out = partial_out.reshape(n_ctx * n_tp, -1, 128).astype(BF)
    square_parts = jnp.concatenate(in_three(squares))
    square_parts = jnp.pad(square_parts, (0, 128 * 4 - square_parts.shape[0])).reshape(1, 4, 128)
    outgoing = jnp.concatenate(
        [partial_out, jnp.broadcast_to(square_parts, (n_ctx * n_tp, 4, 128))], axis=1
    )
    incoming = jnp.sum(exchange(outgoing, BOTH).astype(F32), axis=0)
    out_rows = partial_out.shape[1]
    total = jnp.sum(incoming[out_rows, : 3 * rows].reshape(3, rows), axis=0)
    scale = lax.rsqrt(total / (HEADS * HEAD_DIM) + EPS)
    mixed = incoming[:out_rows].reshape(rows, -1) * scale[:, None]
    return (mixed.reshape(steps, slots, -1).astype(BF), ssm_state)


def solution(mesh):
    return jax.shard_map(
        per_device,
        mesh=mesh,
        in_specs=(
            P(),
            P(),
            P("dp", ("ctx", "tp")),
            P(),
            P(None, ("tp", "ctx"), None, None),
            P(None, ("ctx", "tp")),
            P(None, ("tp", "ctx"), None),
            P(("tp", "ctx"), None),
            P(),
            P(),
            P(("tp", "ctx")),
            P(("tp", "ctx")),
            P(("tp", "ctx")),
            P(("tp", "ctx"), None),
            P(("tp", "ctx"), None, None),
            P("ctx", "dp", "tp", None, None),
            P("ctx", "dp", "tp"),
            P("dp", None, ("tp", "ctx"), None),
            P("dp", None, None),
        ),
        out_specs=(P(None, "dp", ("ctx", "tp")), P("dp", ("tp", "ctx"), None, None)),
        check_vma=False,
    )
```

profile of v0, /device:TPU:1, one launch (start us, length us, event | category | flops | bytes accessed | tf_op | source)
XLA Modules:
  0.0 135.3 jit_solution(1942876022011710154)
XLA Ops:
  0.7 0.9 reshape_squeeze.10
  1.8 1.3 copy.239
  3.3 1.1 fusion.5
  4.5 13.4 %all-to-all-start = ((bf16[16,288,128]{2,1,0:T(8,128)(2,1)}), bf16[16,288,128]{2,1,0:T(8,128)(2,1)S(1)}, u32[]{:S(2)}, u32[]{:S(2)}) async-start(bf16[16,288,128]{2,1,0:T(8,128)(2,1)} %fusion.5), calls=%async_computation | async-start | bytes 2359296 | tf_op jit(solution)/shard_map/all_to_all | solution.py:15
  18.0 0.6 fusion.110
  23.8 0.6 reshape.447
  24.4 0.7 reshape.486
  25.2 0.1 multiply_reduce_fusion.1
  25.5 0.1 copy.237
  25.8 0.8 dynamic_slice.20
  26.6 1.6 %fusion.7 = bf16[64,64]{1,0:T(8,128)(2,1)S(1)} fusion(bf16[6285,64]{0,1:T(8,128)(2,1)} %param.21, s32[64]{0:T(128)S(1)} %sub.53), kind=kOutput, calls=%fused_computation.11 | convolution fusion | flops 51893056 | bytes 812928 | tf_op jit(solution)/shard_map/dot_general | solution.py:76
  28.2 24.6 %psum.7 = bf16[64,64]{1,0:T(8,128)(2,1)S(1)} all-reduce(bf16[64,64]{1,0:T(8,128)(2,1)S(1)} %fusion.7), channel_id=1, replica_groups=mesh['ctx'=16,'dp'=8,'tp'=4] {'dp'}, use_global_device_ids=true, to_apply=%region_1.2 | all-reduce | flops 4096 | bytes 16384 | tf_op jit(solution)/shard_map/psum | solution.py:77
  52.9 11.7 %all-gather = bf16[32,64]{1,0:T(8,128)(2,1)S(1)} all-gather(bf16[8,64]{1,0:T(8,128)(2,1)S(1)} %constant_dynamic-slice_fusion.6), channel_id=2, replica_groups=mesh['ctx'=16,'dp'=8,'tp'=4] {'tp'}, dimensions={0}, use_global_device_ids=true | all-gather | bytes 5120 | tf_op jit(solution)/shard_map/all_gather | solution.py:79
  64.7 2.3 %copy.273 = bf16[4096,128]{1,0:T(8,128)(2,1)} copy(bf16[4096,128]{0,1:T(8,128)(2,1)} %bitcast.343) | data formatting | bytes 2097152 | tf_op jit(solution)/shard_map/dot_general | solution.py:160
  66.9 0.6 reduce_or.9
  67.6 0.6 exponential_negate_fusion
  68.2 0.2 copy.350
  69.1 0.1 convolution_convert_fusion.1
  69.4 0.7 broadcast_in_dim.40
  70.1 10.3 %all-to-all-start.1 = ((bf16[64,10,128]{2,1,0:T(8,128)(2,1)}), bf16[64,10,128]{2,1,0:T(8,128)(2,1)S(1)}, u32[]{:S(2)}, u32[]{:S(2)}) async-start(bf16[64,10,128]{2,1,0:T(8,128)(2,1)} %broadcast_in_dim.40), calls=%async_computation.1 | async-start | bytes 524288 | tf_op jit(solution)/shard_map/all_to_all | solution.py:15
  80.4 0.7 fusion.8
  81.1 0.7 fusion.16
  81.8 1.4 %broadcast_select_fusion = bf16[8,144,128]{2,1,0:T(8,128)(2,1)} fusion(pred[8]{0:T(512)(128)(4,1)} %reduce_or.9, bf16[144,128]{1,0:T(8,128)(2,1)S(1)} %get-tuple-element.31, bf16[144,128]{1,0:T(8,128)(2,1)S(1)} %get-tuple-element.30), kind=kLoop, calls=%fused_computation.15 | loop fusion | flops 147456 | bytes 368648 | tf_op jit(solution)/shard_map/jit(_where)/select_n | solution.py:109
  83.2 9.1 %all-to-all-done.1 = bf16[64,10,128]{2,1,0:T(8,128)(2,1)S(1)} async-done(((bf16[64,10,128]{2,1,0:T(8,128)(2,1)}), bf16[64,10,128]{2,1,0:T(8,128)(2,1)S(1)}, u32[]{:S(2)}, u32[]{:S(2)}) %all-to-all-start.1) | async-done | bytes 163872 | tf_op jit(solution)/shard_map/all_to_all | solution.py:15
  92.4 4.1 %all-to-all-start.2 = ((bf16[8,144,128]{2,1,0:T(8,128)(2,1)}), bf16[8,144,128]{2,1,0:T(8,128)(2,1)}, u32[]{:S(2)}, u32[]{:S(2)}) async-start(bf16[8,144,128]{2,1,0:T(8,128)(2,1)} %broadcast_select_fusion), calls=%async_computation.2 | async-start | bytes 589824 | tf_op jit(solution)/shard_map/all_to_all | solution.py:15
  96.6 0.1 reduce_sum.79
  96.7 0.5 copy-done.16
  97.4 5.7 %reshape.454 = f32[16,4,8,16,6]{4,3,2,1,0:T(8,128)} reshape(f32[64,6,128]{2,1,0:T(8,128)S(1)} %slice_convert_fusion) | data formatting | bytes 393216 | tf_op jit(solution)/shard_map/convert_element_type | solution.py:117
  103.1 2.6 %reduce_sum.76 = f32[4,8,16,6]{3,2,1,0:T(8,128)S(1)} reduce(f32[16,4,8,16,6]{4,3,2,1,0:T(8,128)} %reshape.454, f32[]{:T(128)} %constant.87.clone.1), dimensions={0}, to_apply=%region_2.3 | reduce | flops 46080 | bytes 208900 | tf_op jit(solution)/shard_map/reduce_sum | solution.py:118
  105.7 0.2 copy.243
  105.9 0.3 reshape.444
  106.3 0.6 slice_bitcast_fusion.3
  106.9 0.1 reshape.457
  107.3 1.7 %fusion.18 = f32[8,2,2,64]{3,0,2,1:T(8,128)S(1)} fusion(bf16[2,2,64,4096]{3,2,1,0:T(8,128)(2,1)S(1)} %copy-done, f32[8,4096]{1,0:T(8,128)S(1)} %reshape.456, f32[4096]{0:T(1024)} %param.22, f32[8]{0:T(128)} %copy-done.16), kind=kOutput, calls=%fused_computation.35 | convolution fusion | flops 16875520 | bytes 2252832 | tf_op jit(solution)/shard_map/rd,khed->krhe/dot_general | solution.py:115
  109.1 1.4 %multiply_exponential_fusion.3 = (f32[2,2]{1,0:T(2,128)S(1)}, f32[2,2]{1,0:T(2,128)S(1)}, f32[2,2]{1,0:T(2,128)S(1)}, f32[2,2]{1,0:T(2,128)S(1)}, f32[2,2]{1,0:T...) fusion(f32[2]{0:T(128)} %exponential_negate_fusion, f32[2]{0:T(128)} %param.29, ...), kind=kLoop, calls=%fused_computation.217 | loop fusion | flops 128 | bytes 224 | tf_op jit(solution)/shard_map/exp | solution.py:145
  111.0 0.8 constant_dynamic-slice_fusion.4
  112.0 0.8 broadcast_multiply_fusion.4
  113.0 0.2 fusion.13
  113.2 0.3 fusion.28
  113.5 0.3 fusion.14
  113.8 0.9 multiply_add_fusion
  114.8 0.1 fusion.112
  114.9 0.7 fusion.87
  115.7 0.7 multiply_convert_fusion.2
  116.4 0.9 fusion.6
  117.3 0.1 convert_element_type.166
  117.9 16.4 %all_to_all.20 = bf16[64,8,128]{2,1,0:T(8,128)(2,1)S(1)} all-to-all(bf16[64,8,128]{2,1,0:T(8,128)(2,1)S(1)} %pad_maximum_fusion), channel_id=1, replica_groups=mesh['ctx'=16,'dp'=8,'tp'=4] {'ctx','tp'}, dimensions={0} | all-to-all | bytes 262144 | tf_op jit(solution)/shard_map/all_to_all | solution.py:15
  134.7 0.7 multiply_convert_fusion.3
  (139 shorter events, 4.2 us)
Async XLA Ops:
  0.6 106.7 %copy-start = (bf16[2,2,64,4096]{3,2,1,0:T(8,128)(2,1)S(1)}, bf16[2,2,64,4096]{3,2,1,0:T(8,128)(2,1)}, u32[]{:S(2)}) copy-start(bf16[2,2,64,4096]{3,2,1,0:T(8,128)(2,1)} %param.23) | copy-start | bytes 6291460
  0.6 2.5 %copy-start.3 = (bf16[4096,6]{0,1:T(8,128)(2,1)S(1)}, bf16[4096,6]{0,1:T(8,128)(2,1)}, u32[]{:S(2)}) copy-start(bf16[4096,6]{0,1:T(8,128)(2,1)} %param.24) | copy-start | bytes 147460
  3.3 14.6 %copy-start.19 = (s32[16]{0:T(128)S(1)}, s32[16]{0:T(128)}, u32[]{:S(2)}) copy-start(s32[16]{0:T(128)} %param.20) | copy-start | bytes 196
  3.3 20.5 %copy-start.14 = (bf16[2,3,256]{2,0,1:T(2,128)(2,1)S(1)}, bf16[2,3,256]{2,0,1:T(2,128)(2,1)}, u32[]{:S(2)}) copy-start(bf16[2,3,256]{2,0,1:T(2,128)(2,1)} %param.37) | copy-start | bytes 9220
  3.3 21.1 %copy-start.15 = (bf16[2,3,2,64]{3,2,1,0:T(2,128)(2,1)S(1)}, bf16[2,3,2,64]{3,2,1,0:T(2,128)(2,1)}, u32[]{:S(2)}) copy-start(bf16[2,3,2,64]{3,2,1,0:T(2,128)(2,1)} %param.36) | copy-start | bytes 4612
  3.3 21.9 %copy-start.17 = (s32[4,16]{1,0:T(4,128)S(1)}, s32[4,16]{1,0:T(4,128)}, u32[]{:S(2)}) copy-start(s32[4,16]{1,0:T(4,128)} %param.19) | copy-start | bytes 772
  4.5 63.7 %all-to-all-start = ((bf16[16,288,128]{2,1,0:T(8,128)(2,1)}), bf16[16,288,128]{2,1,0:T(8,128)(2,1)S(1)}, u32[]{:S(2)}, u32[]{:S(2)}) async-start(bf16[16,288,128]{2,1,0:T(8,128)(2,1)} %fusion.5), calls=%async_computation | async-start | bytes 2359296 | tf_op jit(solution)/shard_map/all_to_all | solution.py:15
  17.9 49.7 %copy-start.20 = (f32[2]{0:T(128)S(1)}, f32[2]{0:T(128)}, u32[]{:S(2)}) copy-start(f32[2]{0:T(128)} %param.30) | copy-start | bytes 28
  70.1 22.3 %all-to-all-start.1 = ((bf16[64,10,128]{2,1,0:T(8,128)(2,1)}), bf16[64,10,128]{2,1,0:T(8,128)(2,1)S(1)}, u32[]{:S(2)}, u32[]{:S(2)}) async-start(bf16[64,10,128]{2,1,0:T(8,128)(2,1)} %broadcast_in_dim.40), calls=%async_computation.1 | async-start | bytes 524288 | tf_op jit(solution)/shard_map/all_to_all | solution.py:15
  92.4 18.6 %all-to-all-start.2 = ((bf16[8,144,128]{2,1,0:T(8,128)(2,1)}), bf16[8,144,128]{2,1,0:T(8,128)(2,1)}, u32[]{:S(2)}, u32[]{:S(2)}) async-start(bf16[8,144,128]{2,1,0:T(8,128)(2,1)} %broadcast_select_fusion), calls=%async_computation.2 | async-start | bytes 589824 | tf_op jit(solution)/shard_map/all_to_all | solution.py:15
  96.7 0.5 copy-start.16
  106.3 0.6 copy-start.4
  106.9 3.6 %copy-start.8 = (f32[2,1,256]{2,0,1:T(2,128)S(1)}, f32[2,1,256]{2,0,1:T(2,128)}, u32[]{:S(2)}) copy-start(f32[2,1,256]{2,0,1:T(2,128)} %get-tuple-element.49) | copy-start | bytes 6148
  106.9 3.6 %copy-start.7 = (f32[2,1,256]{2,0,1:T(2,128)S(1)}, f32[2,1,256]{2,0,1:T(2,128)}, u32[]{:S(2)}) copy-start(f32[2,1,256]{2,0,1:T(2,128)} %get-tuple-element.48) | copy-start | bytes 6148
  106.9 3.6 %copy-start.6 = (f32[2,1,256]{2,0,1:T(2,128)S(1)}, f32[2,1,256]{2,0,1:T(2,128)}, u32[]{:S(2)}) copy-start(f32[2,1,256]{2,0,1:T(2,128)} %get-tuple-element.47) | copy-start | bytes 6148
  106.9 3.6 %copy-start.5 = (f32[2,1,256]{2,0,1:T(2,128)S(1)}, f32[2,1,256]{2,0,1:T(2,128)}, u32[]{:S(2)}) copy-start(f32[2,1,256]{2,0,1:T(2,128)} %get-tuple-element.46) | copy-start | bytes 6148
  107.1 4.9 %copy-start.12 = (f32[4,2,64]{2,1,0:T(2,128)S(1)}, f32[4,2,64]{2,1,0:T(2,128)}, u32[]{:S(2)}) copy-start(f32[4,2,64]{2,1,0:T(2,128)} %param.25) | copy-start | bytes 6148
  107.1 5.8 %copy-start.13 = (f32[4,256]{1,0:T(4,128)S(1)}, f32[4,256]{1,0:T(4,128)}, u32[]{:S(2)}) copy-start(f32[4,256]{1,0:T(4,128)} %param.27) | copy-start | bytes 12292
  107.1 5.8 %copy-start.18 = (f32[256]{0:T(256)S(1)}, f32[256]{0:T(256)}, u32[]{:S(2)}) copy-start(f32[256]{0:T(256)} %param.28) | copy-start | bytes 3076
  107.3 9.1 %copy-start.1 = (bf16[4096,128]{1,0:T(8,128)(2,1)S(1)}, bf16[4096,128]{1,0:T(8,128)(2,1)}, u32[]{:S(2)}) copy-start(bf16[4096,128]{1,0:T(8,128)(2,1)} %copy.273) | copy-start | bytes 3145732
  110.5 3.3 %copy-start.9 = (f32[2,2]{1,0:T(2,128)}, f32[2,2]{1,0:T(2,128)S(1)}, u32[]{:S(2)}) copy-start(f32[2,2]{1,0:T(2,128)S(1)} %get-tuple-element.14) | copy-start | bytes 52
  110.5 3.3 %copy-start.10 = (f32[2,2]{1,0:T(2,128)}, f32[2,2]{1,0:T(2,128)S(1)}, u32[]{:S(2)}) copy-start(f32[2,2]{1,0:T(2,128)S(1)} %get-tuple-element.40) | copy-start | bytes 52
  110.5 3.3 %copy-start.11 = (f32[2,2]{1,0:T(2,128)}, f32[2,2]{1,0:T(2,128)S(1)}, u32[]{:S(2)}) copy-start(f32[2,2]{1,0:T(2,128)S(1)} %get-tuple-element.42) | copy-start | bytes 52
  114.7 20.6 %copy-start.2 = (f32[2,2,64,128]{3,2,1,0:T(8,128)}, f32[2,2,64,128]{3,2,1,0:T(8,128)S(1)}, u32[]{:S(2)}) copy-start(f32[2,2,64,128]{3,2,1,0:T(8,128)S(1)} %multiply_add_fusion) | copy-start | bytes 393220
where the time goes:
time: 136 us; the launch traced here: 135 us
  blocking collectives  52.7 us (39%)
  starting transfers between devices  27.8 us (20%)
  local copies, waits for them, and re-layouts  19.7 us (14%)
  other arithmetic  14.2 us (10%)
  waiting for transfers between devices  9.13 us (7%)
  between operations  6.49 us (5%)
  matrix products  5.28 us (4%)
    all_to_all x3, starting transfers between devices, exchange(): return lax.all_to_all(pieces, axis, 0, 0, tiled=True)  27.8 us
    psum x1, blocking collectives, per_device(): found = lax.psum(found, 'dp')  24.6 us
    all_to_all x1, blocking collectives, exchange(): return lax.all_to_all(pieces, axis, 0, 0, tiled=True)  16.4 us
    all_gather x1, blocking collectives, per_device(): beside = lax.all_gather(own, 'tp')  11.7 us
    all_to_all x3, waiting for transfers between devices, exchange(): return lax.all_to_all(pieces, axis, 0, 0, tiled=True)  9.13 us
    convert_element_type x1, local copies, waits for them, and re-layouts, per_device(): everyone[:, own_rows:].reshape(n_ctx, n_tp, rows, n_ctx, own_columns)  5.71 us
  transfers between devices with their start and end apart: 3, of which 1 were waited for; matrix products, arithmetic and copies ran while one was open for 19% of the time, Pallas kernels for 0%

commit v1 on v0

--- a/solution.py
+++ b/solution.py
@@ -2,6 +2,7 @@
 import jax.numpy as jnp
 from jax import lax
 from jax.sharding import PartitionSpec as P
+from jax.lax import all_gather
 
 HEADS = 128
 HEAD_DIM = 64
@@ -74,7 +75,7 @@
     tokens = jnp.swapaxes(tokens.reshape(steps, n_dp, slots), 0, 1).reshape(-1)
     hot = (tokens[:, None] - group * vocab_rows == jnp.arange(vocab_rows)[None, :]).astype(BF)
     found = jnp.dot(hot, embedding, preferred_element_type=F32).astype(BF)
-    found = lax.psum(found, "dp")
+    found = all_gather(found, "dp").sum(axis=0)
     own = lax.dynamic_slice_in_dim(found, group * rows, rows)
     beside = lax.all_gather(own, "tp")
     near = jnp.swapaxes(beside, 0, 1).reshape(rows, block).astype(F32)

time: 136 us -> 133 us (0.978)
  blocking collectives: 52.7 us -> 48.5 us
    psum x1 -> x0, blocking collectives: 24.6 us -> none  [per_device(): found = lax.psum(found, 'dp')]
    all_gather x0 -> x1, blocking collectives: none -> 21.1 us  [per_device(): found = all_gather(found, 'dp').sum(axis=0)]
where the time goes in v1:
time: 133 us; the launch traced here: 132 us
  blocking collectives  48.5 us (36%)
  starting transfers between devices  29 us (22%)
  local copies, waits for them, and re-layouts  19.7 us (15%)
  other arithmetic  14.3 us (11%)
  waiting for transfers between devices  9.13 us (7%)
  between operations  6.49 us (5%)
  matrix products  5.28 us (4%)
    all_to_all x3, starting transfers between devices, exchange(): return lax.all_to_all(pieces, axis, 0, 0, tiled=True)  29 us
    all_gather x1, blocking collectives, per_device(): found = all_gather(found, 'dp').sum(axis=0)  21.1 us
    all_to_all x1, blocking collectives, exchange(): return lax.all_to_all(pieces, axis, 0, 0, tiled=True)  16.5 us
    all_gather x1, blocking collectives, per_device(): beside = lax.all_gather(own, 'tp')  10.9 us
    all_to_all x3, waiting for transfers between devices, exchange(): return lax.all_to_all(pieces, axis, 0, 0, tiled=True)  9.13 us
    convert_element_type x1, local copies, waits for them, and re-layouts, per_device(): everyone[:, own_rows:].reshape(n_ctx, n_tp, rows, n_ctx, own_columns)  5.71 us
  transfers between devices with their start and end apart: 3, of which 1 were waited for; matrix products, arithmetic and copies ran while one was open for 19% of the time, Pallas kernels for 0%

profile of v1, /device:TPU:1, one launch (start us, length us, event | category | flops | bytes accessed | tf_op | source)
XLA Modules:
  0.0 132.4 jit_solution(2021530369447569469)
XLA Ops:
  0.7 0.9 reshape_squeeze.10
  1.8 1.3 copy.238
  3.3 1.1 fusion.5
  4.5 13.4 %all-to-all-start = ((bf16[16,288,128]{2,1,0:T(8,128)(2,1)}), bf16[16,288,128]{2,1,0:T(8,128)(2,1)S(1)}, u32[]{:S(2)}, u32[]{:S(2)}) async-start(bf16[16,288,128]{2,1,0:T(8,128)(2,1)} %fusion.5), calls=%async_computation | async-start | bytes 2359296 | tf_op jit(solution)/shard_map/all_to_all | solution.py:16
  18.0 0.6 fusion.110
  23.8 0.6 reshape.447
  24.4 0.7 reshape.487
  25.2 0.1 multiply_reduce_fusion.1
  25.5 0.1 copy.236
  25.8 0.8 dynamic_slice.20
  26.6 1.6 %fusion.7 = bf16[64,64]{1,0:T(8,128)(2,1)S(1)} fusion(bf16[6285,64]{0,1:T(8,128)(2,1)} %param.21, s32[64]{0:T(128)S(1)} %sub.53), kind=kOutput, calls=%fused_computation.11 | convolution fusion | flops 51893056 | bytes 812928 | tf_op jit(solution)/shard_map/dot_general | solution.py:77
  28.2 21.1 %all-gather = bf16[512,64]{1,0:T(8,128)(2,1)S(1)} all-gather(bf16[64,64]{1,0:T(8,128)(2,1)S(1)} %fusion.7), channel_id=2, replica_groups=mesh['ctx'=16,'dp'=8,'tp'=4] {'dp'}, dimensions={0}, use_global_device_ids=true | all-gather | bytes 73728 | tf_op jit(solution)/shard_map/all_gather | solution.py:78
  49.4 10.9 %all-gather.1 = bf16[32,64]{1,0:T(8,128)(2,1)S(1)} all-gather(bf16[8,64]{1,0:T(8,128)(2,1)S(1)} %constant_dynamic-slice_fusion.6), channel_id=3, replica_groups=mesh['ctx'=16,'dp'=8,'tp'=4] {'tp'}, dimensions={0}, use_global_device_ids=true | all-gather | bytes 5120 | tf_op jit(solution)/shard_map/all_gather | solution.py:80
  60.5 2.3 %copy.272 = bf16[4096,128]{1,0:T(8,128)(2,1)} copy(bf16[4096,128]{0,1:T(8,128)(2,1)} %bitcast.344) | data formatting | bytes 2097152 | tf_op jit(solution)/shard_map/dot_general | solution.py:161
  62.8 0.6 reduce_or.9
  63.4 0.6 exponential_negate_fusion
  64.0 0.2 copy.349
  64.9 0.1 convolution_convert_fusion.1
  65.2 0.7 broadcast_in_dim.40
  65.9 10.3 %all-to-all-start.1 = ((bf16[64,10,128]{2,1,0:T(8,128)(2,1)}), bf16[64,10,128]{2,1,0:T(8,128)(2,1)S(1)}, u32[]{:S(2)}, u32[]{:S(2)}) async-start(bf16[64,10,128]{2,1,0:T(8,128)(2,1)} %broadcast_in_dim.40), calls=%async_computation.1 | async-start | bytes 524288 | tf_op jit(solution)/shard_map/all_to_all | solution.py:16
  76.3 0.7 fusion.8
  77.0 0.7 fusion.16
  77.7 1.4 %broadcast_select_fusion = bf16[8,144,128]{2,1,0:T(8,128)(2,1)} fusion(pred[8]{0:T(512)(128)(4,1)} %reduce_or.9, bf16[144,128]{1,0:T(8,128)(2,1)S(1)} %get-tuple-element.31, bf16[144,128]{1,0:T(8,128)(2,1)S(1)} %get-tuple-element.30), kind=kLoop, calls=%fused_computation.15 | loop fusion | flops 147456 | bytes 368648 | tf_op jit(solution)/shard_map/jit(_where)/select_n | solution.py:110
  79.1 9.1 %all-to-all-done.1 = bf16[64,10,128]{2,1,0:T(8,128)(2,1)S(1)} async-done(((bf16[64,10,128]{2,1,0:T(8,128)(2,1)}), bf16[64,10,128]{2,1,0:T(8,128)(2,1)S(1)}, u32[]{:S(2)}, u32[]{:S(2)}) %all-to-all-start.1) | async-done | bytes 163872 | tf_op jit(solution)/shard_map/all_to_all | solution.py:16
  88.3 5.2 %all-to-all-start.2 = ((bf16[8,144,128]{2,1,0:T(8,128)(2,1)}), bf16[8,144,128]{2,1,0:T(8,128)(2,1)}, u32[]{:S(2)}, u32[]{:S(2)}) async-start(bf16[8,144,128]{2,1,0:T(8,128)(2,1)} %broadcast_select_fusion), calls=%async_computation.2 | async-start | bytes 589824 | tf_op jit(solution)/shard_map/all_to_all | solution.py:16
  93.7 0.1 reduce_sum.92
  93.8 0.5 copy-done.16
  94.5 5.7 %reshape.454 = f32[16,4,8,16,6]{4,3,2,1,0:T(8,128)} reshape(f32[64,6,128]{2,1,0:T(8,128)S(1)} %slice_convert_fusion) | data formatting | bytes 393216 | tf_op jit(solution)/shard_map/convert_element_type | solution.py:118
  100.2 2.6 %reduce_sum.89 = f32[4,8,16,6]{3,2,1,0:T(8,128)S(1)} reduce(f32[16,4,8,16,6]{4,3,2,1,0:T(8,128)} %reshape.454, f32[]{:T(128)} %constant.88.clone.1), dimensions={0}, to_apply=%region_2.3 | reduce | flops 46080 | bytes 208900 | tf_op jit(solution)/shard_map/reduce_sum | solution.py:119
  102.8 0.2 copy.242
  103.0 0.3 reshape.444
  103.3 0.6 slice_bitcast_fusion.3
  104.0 0.1 reshape.457
  104.4 1.7 %fusion.18 = f32[8,2,2,64]{3,0,2,1:T(8,128)S(1)} fusion(bf16[2,2,64,4096]{3,2,1,0:T(8,128)(2,1)S(1)} %copy-done, f32[8,4096]{1,0:T(8,128)S(1)} %reshape.456, f32[4096]{0:T(1024)} %param.22, f32[8]{0:T(128)} %copy-done.16), kind=kOutput, calls=%fused_computation.35 | convolution fusion | flops 16875520 | bytes 2252832 | tf_op jit(solution)/shard_map/rd,khed->krhe/dot_general | solution.py:116
  106.1 1.4 %multiply_exponential_fusion.3 = (f32[2,2]{1,0:T(2,128)S(1)}, f32[2,2]{1,0:T(2,128)S(1)}, f32[2,2]{1,0:T(2,128)S(1)}, f32[2,2]{1,0:T(2,128)S(1)}, f32[2,2]{1,0:T...) fusion(f32[2]{0:T(128)} %exponential_negate_fusion, f32[2]{0:T(128)} %param.29, ...), kind=kLoop, calls=%fused_computation.216 | loop fusion | flops 128 | bytes 224 | tf_op jit(solution)/shard_map/exp | solution.py:146
  108.0 0.8 constant_dynamic-slice_fusion.4
  109.1 0.8 broadcast_multiply_fusion.4
  110.1 0.2 fusion.13
  110.3 0.3 fusion.28
  110.6 0.3 fusion.14
  110.9 0.9 multiply_add_fusion
  111.8 0.1 fusion.112
  112.0 0.7 fusion.87
  112.7 0.7 multiply_convert_fusion.2
  113.5 0.9 fusion.6
  114.4 0.1 convert_element_type.168
  114.9 16.5 %all_to_all.20 = bf16[64,8,128]{2,1,0:T(8,128)(2,1)S(1)} all-to-all(bf16[64,8,128]{2,1,0:T(8,128)(2,1)S(1)} %pad_maximum_fusion), channel_id=1, replica_groups=mesh['ctx'=16,'dp'=8,'tp'=4] {'ctx','tp'}, dimensions={0} | all-to-all | bytes 262144 | tf_op jit(solution)/shard_map/all_to_all | solution.py:16
  131.8 0.7 multiply_convert_fusion.3
  (140 shorter events, 4.2 us)
Async XLA Ops:
  0.6 103.7 %copy-start = (bf16[2,2,64,4096]{3,2,1,0:T(8,128)(2,1)S(1)}, bf16[2,2,64,4096]{3,2,1,0:T(8,128)(2,1)}, u32[]{:S(2)}) copy-start(bf16[2,2,64,4096]{3,2,1,0:T(8,128)(2,1)} %param.23) | copy-start | bytes 6291460
  0.6 2.5 %copy-start.3 = (bf16[4096,6]{0,1:T(8,128)(2,1)S(1)}, bf16[4096,6]{0,1:T(8,128)(2,1)}, u32[]{:S(2)}) copy-start(bf16[4096,6]{0,1:T(8,128)(2,1)} %param.24) | copy-start | bytes 147460
  3.3 14.6 %copy-start.19 = (s32[16]{0:T(128)S(1)}, s32[16]{0:T(128)}, u32[]{:S(2)}) copy-start(s32[16]{0:T(128)} %param.20) | copy-start | bytes 196
  3.3 20.5 %copy-start.14 = (bf16[2,3,256]{2,0,1:T(2,128)(2,1)S(1)}, bf16[2,3,256]{2,0,1:T(2,128)(2,1)}, u32[]{:S(2)}) copy-start(bf16[2,3,256]{2,0,1:T(2,128)(2,1)} %param.37) | copy-start | bytes 9220
  3.3 21.1 %copy-start.15 = (bf16[2,3,2,64]{3,2,1,0:T(2,128)(2,1)S(1)}, bf16[2,3,2,64]{3,2,1,0:T(2,128)(2,1)}, u32[]{:S(2)}) copy-start(bf16[2,3,2,64]{3,2,1,0:T(2,128)(2,1)} %param.36) | copy-start | bytes 4612
  3.3 21.9 %copy-start.17 = (s32[4,16]{1,0:T(4,128)S(1)}, s32[4,16]{1,0:T(4,128)}, u32[]{:S(2)}) copy-start(s32[4,16]{1,0:T(4,128)} %param.19) | copy-start | bytes 772
  4.5 59.5 %all-to-all-start = ((bf16[16,288,128]{2,1,0:T(8,128)(2,1)}), bf16[16,288,128]{2,1,0:T(8,128)(2,1)S(1)}, u32[]{:S(2)}, u32[]{:S(2)}) async-start(bf16[16,288,128]{2,1,0:T(8,128)(2,1)} %fusion.5), calls=%async_computation | async-start | bytes 2359296 | tf_op jit(solution)/shard_map/all_to_all | solution.py:16
  17.9 45.5 %copy-start.20 = (f32[2]{0:T(128)S(1)}, f32[2]{0:T(128)}, u32[]{:S(2)}) copy-start(f32[2]{0:T(128)} %param.30) | copy-start | bytes 28
  65.9 22.4 %all-to-all-start.1 = ((bf16[64,10,128]{2,1,0:T(8,128)(2,1)}), bf16[64,10,128]{2,1,0:T(8,128)(2,1)S(1)}, u32[]{:S(2)}, u32[]{:S(2)}) async-start(bf16[64,10,128]{2,1,0:T(8,128)(2,1)} %broadcast_in_dim.40), calls=%async_computation.1 | async-start | bytes 524288 | tf_op jit(solution)/shard_map/all_to_all | solution.py:16
  88.3 19.8 %all-to-all-start.2 = ((bf16[8,144,128]{2,1,0:T(8,128)(2,1)}), bf16[8,144,128]{2,1,0:T(8,128)(2,1)}, u32[]{:S(2)}, u32[]{:S(2)}) async-start(bf16[8,144,128]{2,1,0:T(8,128)(2,1)} %broadcast_select_fusion), calls=%async_computation.2 | async-start | bytes 589824 | tf_op jit(solution)/shard_map/all_to_all | solution.py:16
  93.8 0.5 copy-start.16
  103.3 0.6 copy-start.4
  104.0 3.6 %copy-start.8 = (f32[2,1,256]{2,0,1:T(2,128)S(1)}, f32[2,1,256]{2,0,1:T(2,128)}, u32[]{:S(2)}) copy-start(f32[2,1,256]{2,0,1:T(2,128)} %get-tuple-element.49) | copy-start | bytes 6148
  104.0 3.6 %copy-start.7 = (f32[2,1,256]{2,0,1:T(2,128)S(1)}, f32[2,1,256]{2,0,1:T(2,128)}, u32[]{:S(2)}) copy-start(f32[2,1,256]{2,0,1:T(2,128)} %get-tuple-element.48) | copy-start | bytes 6148
  104.0 3.6 %copy-start.6 = (f32[2,1,256]{2,0,1:T(2,128)S(1)}, f32[2,1,256]{2,0,1:T(2,128)}, u32[]{:S(2)}) copy-start(f32[2,1,256]{2,0,1:T(2,128)} %get-tuple-element.47) | copy-start | bytes 6148
  104.0 3.6 %copy-start.5 = (f32[2,1,256]{2,0,1:T(2,128)S(1)}, f32[2,1,256]{2,0,1:T(2,128)}, u32[]{:S(2)}) copy-start(f32[2,1,256]{2,0,1:T(2,128)} %get-tuple-element.46) | copy-start | bytes 6148
  104.1 4.9 %copy-start.12 = (f32[4,2,64]{2,1,0:T(2,128)S(1)}, f32[4,2,64]{2,1,0:T(2,128)}, u32[]{:S(2)}) copy-start(f32[4,2,64]{2,1,0:T(2,128)} %param.25) | copy-start | bytes 6148
  104.2 5.8 %copy-start.13 = (f32[4,256]{1,0:T(4,128)S(1)}, f32[4,256]{1,0:T(4,128)}, u32[]{:S(2)}) copy-start(f32[4,256]{1,0:T(4,128)} %param.27) | copy-start | bytes 12292
  104.2 5.8 %copy-start.18 = (f32[256]{0:T(256)S(1)}, f32[256]{0:T(256)}, u32[]{:S(2)}) copy-start(f32[256]{0:T(256)} %param.28) | copy-start | bytes 3076
  104.4 9.1 %copy-start.1 = (bf16[4096,128]{1,0:T(8,128)(2,1)S(1)}, bf16[4096,128]{1,0:T(8,128)(2,1)}, u32[]{:S(2)}) copy-start(bf16[4096,128]{1,0:T(8,128)(2,1)} %copy.272) | copy-start | bytes 3145732
  107.5 3.3 %copy-start.9 = (f32[2,2]{1,0:T(2,128)}, f32[2,2]{1,0:T(2,128)S(1)}, u32[]{:S(2)}) copy-start(f32[2,2]{1,0:T(2,128)S(1)} %get-tuple-element.14) | copy-start | bytes 52
  107.6 3.3 %copy-start.10 = (f32[2,2]{1,0:T(2,128)}, f32[2,2]{1,0:T(2,128)S(1)}, u32[]{:S(2)}) copy-start(f32[2,2]{1,0:T(2,128)S(1)} %get-tuple-element.40) | copy-start | bytes 52
  107.6 3.3 %copy-start.11 = (f32[2,2]{1,0:T(2,128)}, f32[2,2]{1,0:T(2,128)S(1)}, u32[]{:S(2)}) copy-start(f32[2,2]{1,0:T(2,128)S(1)} %get-tuple-element.42) | copy-start | bytes 52
  111.8 20.6 %copy-start.2 = (f32[2,2,64,128]{3,2,1,0:T(8,128)}, f32[2,2,64,128]{3,2,1,0:T(8,128)S(1)}, u32[]{:S(2)}) copy-start(f32[2,2,64,128]{3,2,1,0:T(8,128)S(1)} %multiply_add_fusion) | copy-start | bytes 393220
